TPU v7x, 256 devices: a whole 4x4x8 slice. The times are simulated.
256 devices in a mesh: va: 8 (over z_hi, y), vb: 4 (over z_lo), oj: 8 (over x, core).
Axes of the slice: x: 4, y: 4, z: 8 (z_hi: 2, z_lo: 4; z = z_hi * 4 + z_lo), core: 2. Of those that a mesh axis runs over, the one named last changes fastest.
Arguments:
- occ_slab: bfloat16 [3584, 2, 2048], P(('vb', 'oj'), None, 'va'), may hold values from -0.875 to 0.875
- pair_slab: bfloat16 [3584, 8, 2048], P(('va', 'oj'), None, 'vb'), may hold values from -0.875 to 0.875
- occ_energy: float32 [2], replicated, may hold values from -1.5 to -0.3
- pair_energy: float32 [8], P('oj'), may hold values from -1.5 to -0.3
- vir_energy: float32 [2048], replicated, may hold values from 0.2 to 3
Outputs:
- gamma_occ: float32 [3584, 2, 2048], P(('vb', 'oj'), None, 'va')
- gamma_pair: float32 [3584, 8, 2048], P('va', 'oj', 'vb')
All inputs are finite; a program needn't handle non-finite values.
Results may differ from a plain program's by a relative error of at most 0.002.
Values may be sent and summed in bfloat16 or wider, within the bound.
A program may use at most 128 MiB of HBM per device.

v0:
```python
import jax
import jax.numpy as jnp
from jax import lax
from jax.sharding import PartitionSpec as P


def per_device(occ_slab, pair_slab, occ_energy, pair_energy, vir_energy):
    occ_full = lax.all_gather(occ_slab, ("vb", "oj"), axis=0, tiled=True)
    collected = lax.all_gather(pair_slab, "va", axis=0, tiled=True)
    mingled = lax.all_to_all(collected, "oj", split_axis=1, concat_axis=0, tiled=True)
    va_count = lax.axis_size("va")
    oj_count = lax.axis_size("oj")
    shaped = mingled.reshape(oj_count, va_count, -1, mingled.shape[1], mingled.shape[2])
    pair_full = jnp.swapaxes(shaped, 0, 1).reshape(-1, mingled.shape[1], mingled.shape[2])
    width_a = occ_full.shape[2]
    width_b = pair_full.shape[2]
    energy_a = lax.dynamic_slice_in_dim(vir_energy, lax.axis_index("va") * width_a, width_a)
    energy_b = lax.dynamic_slice_in_dim(vir_energy, lax.axis_index("vb") * width_b, width_b)
    pair_ints = jnp.einsum("qia,qjb->ijab", occ_full, pair_full, preferred_element_type=jnp.float32)
    denominator = (
        occ_energy[:, None, None, None]
        + pair_energy[None, :, None, None]
        - energy_a[None, None, :, None]
        - energy_b[None, None, None, :]
    )
    amplitudes = (pair_ints / denominator).astype(jnp.bfloat16)
    gamma_occ = lax.psum_scatter(
        jnp.einsum("ijab,qjb->qia", amplitudes, pair_full, preferred_element_type=jnp.float32),
        ("vb", "oj"),
        scatter_dimension=0,
        tiled=True,
    )
    gamma_pair = lax.psum_scatter(
        jnp.einsum("ijab,qia->qjb", amplitudes, occ_full, preferred_element_type=jnp.float32),
        "va",
        scatter_dimension=0,
        tiled=True,
    )
    return (gamma_occ, gamma_pair)


def solution(mesh):
    placed = (P(("vb", "oj"), None, "va"), P(("va", "oj"), None, "vb"), P(), P("oj"), P())
    return jax.shard_map(
        per_device,
        mesh=mesh,
        in_specs=placed,
        out_specs=(P(("vb", "oj"), None, "va"), P("va", "oj", "vb")),
        check_vma=False,
    )
```

profile of v0, /device:TPU:1, one launch (start us, length us, event | category | flops | bytes accessed | tf_op | source)
XLA Modules:
  0.0 833.1 jit_solution(16251034097933430811)
XLA Ops:
  7.2 0.0 all-gather.3.cloned.1.call-start
  7.2 1.9 copy.25
  9.1 0.0 all-gather.3.cloned.1.call-update
  9.2 0.0 all-gather.5.cloned.1.call-start
  9.2 1.6 copy.27
  10.8 0.0 all-gather.5.cloned.1.call-update
  10.8 0.0 copy-start.1
  10.8 103.1 %all-gather.3.cloned.1.call-done = bf16[448,8,512]{2,0,1:T(8,128)(2,1)} async-done(((bf16[56,8,512]{2,0,1:T(8,128)(2,1)}), bf16[448,8,512]{2,0,1:T(8,128)(2,1)}) %all-gather.3.cloned.1.call-update) | async-done | bytes 3670032 | tf_op jit(solution)/shard_map/all_gather | solution.py:9
  113.9 5.5 all-to-all-start
  119.4 0.0 all-reduce.7.cloned.1.call-start
  120.1 0.8 dynamic_slice.6
  120.8 0.8 dynamic_slice.7
  121.6 0.0 copy-done.1
  121.6 0.1 broadcast_subtract_fusion
  121.7 55.0 %all-to-all-done = bf16[448,8,512]{2,0,1:T(8,128)(2,1)} async-done(((bf16[448,8,512]{2,0,1:T(8,128)(2,1)}), bf16[448,8,512]{2,0,1:T(8,128)(2,1)}, u32[]{:S(2)}, u32[]{:S(2)}) %all-to-all-start) | async-done | bytes 3670048 | tf_op jit(solution)/shard_map/all_to_all | solution.py:10
  176.7 4.2 copy.26
  180.9 11.5 %all-gather.5.cloned.1.call-done = bf16[3584,2,256]{2,0,1:T(8,128)(2,1)} async-done(((bf16[112,2,256]{2,0,1:T(8,128)(2,1)}), bf16[3584,2,256]{2,0,1:T(8,128)(2,1)}) %all-gather.5.cloned.1.call-update) | async-done | bytes 3670032 | tf_op jit(solution)/shard_map/all_gather | solution.py:8
  192.5 5.4 fusion.2
  197.9 5.1 convolution_bitcast_fusion
  203.0 16.6 %copy.31 = f32[3584,1,512]{2,1,0:T(1,128)} copy(f32[3584,1,512]{0,2,1:T(8,128)} %convolution_bitcast_fusion) | data formatting | bytes 14680064 | tf_op jit(solution)/shard_map/ijab,qia->qjb/dot_general | solution.py:34
  219.6 0.0 all-reduce.7.cloned.1.call-update
  219.7 0.0 all-reduce.5.cloned.1.call-start
  219.7 7.1 convolution_bitcast_fusion.1
  226.8 11.7 %copy.30 = f32[3584,2,256]{2,1,0:T(2,128)} copy(f32[3584,2,256]{0,2,1:T(8,128)} %convolution_bitcast_fusion.1) | data formatting | bytes 14680064 | tf_op jit(solution)/shard_map/ijab,qjb->qia/dot_general | solution.py:28
  238.6 0.0 all-reduce.5.cloned.1.call-update
  238.6 0.6 copy-done.3
  239.2 0.6 dynamic-slice.2
  239.8 0.6 dynamic-slice
  241.7 289.5 %all-reduce.7.cloned.1.call-done = f32[3584,1,512]{2,1,0:T(1,128)} async-done(((f32[3584,1,512]{2,1,0:T(1,128)}), f32[3584,1,512]{2,1,0:T(1,128)}) %all-reduce.7.cloned.1.call-update) | async-done | bytes 7340048
  531.2 2.7 constant_dynamic-slice_fusion
  533.9 291.0 %all-reduce.5.cloned.1.call-done = f32[3584,2,256]{2,1,0:T(2,128)} async-done(((f32[3584,2,256]{2,1,0:T(2,128)}), f32[3584,2,256]{2,1,0:T(2,128)}) %all-reduce.5.cloned.1.call-update) | async-done | bytes 7340048
  824.9 1.6 constant_dynamic-slice_fusion.1
  (6 shorter events, 0.0 us)
Async XLA Ops:
  7.2 106.8 %all-gather.3.cloned.1.call-start = ((), (), s32[]{:S(2)}) async-start(), calls=%async_computation.1 | async-start | bytes 4128768 | tf_op jit(solution)/shard_map/all_gather | solution.py:9
  9.2 183.3 %all-gather.5.cloned.1.call-start = ((), (), s32[]{:S(2)}) async-start(), calls=%async_computation.2 | async-start | bytes 3784704 | tf_op jit(solution)/shard_map/all_gather | solution.py:8
  10.8 110.8 %copy-start.1 = (f32[2]{0:T(128)S(1)}, f32[2]{0:T(128)}, u32[]{:S(2)}) copy-start(f32[2]{0:T(128)} %param.7) | copy-start | bytes 28
  113.9 62.8 %all-to-all-start = ((bf16[448,8,512]{2,0,1:T(8,128)(2,1)}), bf16[448,8,512]{2,0,1:T(8,128)(2,1)}, u32[]{:S(2)}, u32[]{:S(2)}) async-start(bf16[448,8,512]{2,0,1:T(8,128)(2,1)} %all-gather.3.cloned.1.call-done), calls=%async_computation | async-start | bytes 7340032 | tf_op jit(solution)/shard_map/all_to_all | solution.py:10
  119.4 411.8 %all-reduce.7.cloned.1.call-start = ((), (), s32[]{:S(2)}) async-start(), calls=%async_computation.4 | async-start | bytes 14680064
  192.5 5.4 copy-start
  219.7 605.3 %all-reduce.5.cloned.1.call-start = ((), (), s32[]{:S(2)}) async-start(), calls=%async_computation.3 | async-start | bytes 14680064
  238.6 0.7 copy-start.3
  238.6 1.3 copy-start.2
Sparse Core Ops, SparseCore 0:
  11.1 102.7 all-gather.2
  116.3 76.1 all-gather.4
  219.8 311.3 all-reduce.6
  533.7 291.1 all-reduce.4
where the time goes:
time: 834 us; the launch traced here: 833 us
  waiting for transfers between devices  750 us (90%)
  local copies, waits for them, and re-layouts  43.8 us (5%)
  matrix products  17.6 us (2%)
  between operations  15.7 us (2%)
    unnamed x6, waiting for transfers between devices  581 us
    all_gather x1, waiting for transfers between devices, per_device(): collected = lax.all_gather(pair_slab, 'va', axis=0, tiled=True)  103 us
    all_to_all x1, waiting for transfers between devices, per_device(): lax.all_to_all(collected, 'oj', split_axis=1, concat_axis=0, tiled=True)  55 us
  transfers between devices with their start and end apart: 5, of which 5 were waited for; matrix products, arithmetic and copies ran while one was open for 4% of the time, Pallas kernels for 0%

commit v1 on v0

--- a/solution.py
+++ b/solution.py
@@ -7,7 +7,10 @@
 def per_device(occ_slab, pair_slab, occ_energy, pair_energy, vir_energy):
     occ_full = lax.all_gather(occ_slab, ("vb", "oj"), axis=0, tiled=True)
     collected = lax.all_gather(pair_slab, "va", axis=0, tiled=True)
-    mingled = lax.all_to_all(collected, "oj", split_axis=1, concat_axis=0, tiled=True)
+    mingled = jnp.concatenate(
+        lax.all_to_all(jnp.stack(jnp.split(collected, lax.axis_size("oj"), axis=1)), "oj", 0, 0),
+        axis=0,
+    )
     va_count = lax.axis_size("va")
     oj_count = lax.axis_size("oj")
     shaped = mingled.reshape(oj_count, va_count, -1, mingled.shape[1], mingled.shape[2])

time: 834 us -> 696 us (0.83)
  waiting for transfers between devices: 750 us -> 605 us
    unnamed x6 -> x5, waiting for transfers between devices: 581 us -> 305 us
    reduce_scatter x0 -> x1, waiting for transfers between devices: none -> 144 us  [per_device(): lax.psum_scatter(jnp.einsum('ijab,qjb->qia', amplitudes, pair_full, prefe...]
    unnamed x14 -> x18, local copies, waits for them, and re-layouts: 9.68 us -> 22.1 us
    dot_general x1 -> x0, local copies, waits for them, and re-layouts: 11.7 us -> none  [per_device(): jnp.einsum('ijab,qjb->qia', amplitudes, pair_full, preferred_element_type...]
    all_gather x1, waiting for transfers between devices: 11.5 us -> 0.01 us  [per_device(): occ_full = lax.all_gather(occ_slab, ('vb', 'oj'), axis=0, tiled=True)]
  transfers between devices with their start and end apart: 5 -> 5, of which waited for: 5 -> 4; matrix products, arithmetic and copies ran while one was open for 4% -> 5% of each run, Pallas kernels for 0% -> 0%
where the time goes in v1:
time: 696 us; the launch traced here: 690 us
  waiting for transfers between devices  605 us (87%)
  local copies, waits for them, and re-layouts  46.4 us (7%)
  matrix products  17.5 us (3%)
  between operations  15.1 us (2%)
    unnamed x5, waiting for transfers between devices  305 us
    reduce_scatter x1, waiting for transfers between devices, per_device(): lax.psum_scatter(jnp.einsum('ijab,qjb->qia', amplitudes, pair_full, prefe...  144 us
    all_gather x1, waiting for transfers between devices, per_device(): collected = lax.all_gather(pair_slab, 'va', axis=0, tiled=True)  103 us
    all_to_all x1, waiting for transfers between devices, per_device(): lax.all_to_all(jnp.stack(jnp.split(collected, lax.axis_size('oj'), axis=1...  53.4 us
    unnamed x18, local copies, waits for them, and re-layouts  22.1 us
    dot_general x1, local copies, waits for them, and re-layouts, per_device(): jnp.einsum('ijab,qia->qjb', amplitudes, occ_full, preferred_element_type=...  16.6 us
  transfers between devices with their start and end apart: 5, of which 4 were waited for; matrix products, arithmetic and copies ran while one was open for 5% of the time, Pallas kernels for 0%

profile of v1, /device:TPU:1, one launch (start us, length us, event | category | flops | bytes accessed | tf_op | source)
XLA Modules:
  0.0 689.9 jit_solution(5624880349592561552)
XLA Ops:
  7.2 0.0 all-gather.3.cloned.1.call-start
  7.2 1.9 copy.27
  9.1 0.0 all-gather.3.cloned.1.call-update
  9.2 0.0 all-gather.5.cloned.1.call-start
  9.2 1.6 copy.29
  10.8 0.0 all-gather.5.cloned.1.call-update
  10.8 103.2 %all-gather.3.cloned.1.call-done = bf16[448,8,512]{2,0,1:T(8,128)(2,1)} async-done(((bf16[56,8,512]{2,0,1:T(8,128)(2,1)}), bf16[448,8,512]{2,0,1:T(8,128)(2,1)}) %all-gather.3.cloned.1.call-update) | async-done | bytes 3670032 | tf_op jit(solution)/shard_map/all_gather | solution.py:9
  113.9 1.8 fusion.10
  115.8 1.9 fusion.9
  117.6 1.9 fusion.8
  119.5 1.9 fusion.7
  121.4 1.8 fusion.6
  123.2 1.8 fusion.5
  125.0 1.8 fusion.4
  126.8 1.8 fusion.3
  128.7 5.6 all-to-all-start
  134.3 0.8 dynamic_slice.7
  135.0 0.8 dynamic_slice.6
  136.5 0.1 broadcast_subtract_fusion
  136.5 53.4 %all-to-all-done = bf16[8,448,1,512]{3,1,2,0:T(8,128)(2,1)} async-done(((bf16[8,448,1,512]{3,1,2,0:T(8,128)(2,1)}), bf16[8,448,1,512]{3,1,2,0:T(8,128)(2,1)}, u32[]{:S(2)}, u32[]{:S(2)}) %all-to-all-start) | async-done | bytes 3670048 | tf_op jit(solution)/shard_map/all_to_all | solution.py:11
  189.9 4.3 copy.28
  194.2 5.4 fusion.2
  199.6 5.1 convolution_bitcast_fusion
  204.7 16.6 %copy.32 = f32[3584,1,512]{2,1,0:T(1,128)} copy(f32[3584,1,512]{0,2,1:T(8,128)} %convolution_bitcast_fusion) | data formatting | bytes 14680064 | tf_op jit(solution)/shard_map/ijab,qia->qjb/dot_general | solution.py:37
  221.4 0.0 reduce-scatter.2.cloned.1.call-start
  221.4 7.0 %fusion.11 = f32[3584,2,256]{2,0,1:T(8,128)} fusion(bf16[3584,512,1]{1,0,2:T(8,128)(2,1)} %bitcast.67, bf16[2,256,512]{1,2,0:T(8,128)(2,1)S(1)} %fusion.2), kind=kOutput, calls=%fused_computation.24 | convolution fusion | flops 1879048192 | bytes 11534336 | tf_op jit(solution)/shard_map/ijab,qjb->qia/dot_general | solution.py:31
  228.5 0.6 copy-done.2
  229.1 0.6 dynamic-slice
  230.4 304.7 %all-reduce.3.cloned.1.call-done = f32[3584,1,512]{2,1,0:T(1,128)} async-done(((f32[3584,1,512]{2,1,0:T(1,128)}), f32[3584,1,512]{2,1,0:T(1,128)}) %all-reduce.3.cloned.1.call-update) | async-done | bytes 7340048
  535.0 2.7 constant_dynamic-slice_fusion
  537.8 143.8 %reduce-scatter.2.cloned.1.call-done = f32[112,2,256]{2,0,1:T(8,128)} async-done(((f32[3584,2,256]{2,0,1:T(8,128)}), f32[112,2,256]{2,0,1:T(8,128)}) %reduce-scatter.2.cloned.1.call-update) | async-done | bytes 229392 | tf_op jit(solution)/shard_map/reduce_scatter | solution.py:30
  681.5 1.8 copy.33
  (10 shorter events, 0.0 us)
Async XLA Ops:
  7.2 106.8 %all-gather.3.cloned.1.call-start = ((), (), s32[]{:S(2)}) async-start(), calls=%async_computation.2 | async-start | bytes 4128768 | tf_op jit(solution)/shard_map/all_gather | solution.py:9
  9.2 185.0 %all-gather.5.cloned.1.call-start = ((), (), s32[]{:S(2)}) async-start(), calls=%async_computation.3 | async-start | bytes 3784704 | tf_op jit(solution)/shard_map/all_gather | solution.py:8
  128.7 7.8 %copy-start.1 = (f32[2]{0:T(128)S(1)}, f32[2]{0:T(128)}, u32[]{:S(2)}) copy-start(f32[2]{0:T(128)} %param.7) | copy-start | bytes 28
  128.7 61.2 %all-to-all-start = ((bf16[8,448,1,512]{3,1,2,0:T(8,128)(2,1)}), bf16[8,448,1,512]{3,1,2,0:T(8,128)(2,1)}, u32[]{:S(2)}, u32[]{:S(2)}) async-start(bf16[8,448,1,512]{3,1,2,0:T(8,128)(2,1)} %fusion.3), calls=%async_computation | async-start | bytes 7340032 | tf_op jit(solution)/shard_map/all_to_all | solution.py:11
  134.3 400.8 %all-reduce.3.cloned.1.call-start = ((), (), s32[]{:S(2)}) async-start(), calls=%async_computation.5 | async-start | bytes 14680064
  194.2 5.4 copy-start
  221.4 460.1 %reduce-scatter.2.cloned.1.call-start = ((), (), s32[]{:S(2)}) async-start(), calls=%async_computation.4 | async-start | bytes 7569408 | tf_op jit(solution)/shard_map/reduce_scatter | solution.py:30
  228.5 0.7 copy-start.2
Sparse Core Ops, SparseCore 0:
  11.1 102.7 all-gather.2
  116.3 77.3 all-gather.4
  221.5 313.4 all-reduce.2
  537.5 144.0 reduce-scatter.1
